TPU v7x, 512 devices: a whole 4x8x8 slice. The times are simulated.
512 devices in a mesh: seq: 32 (over y, x), head: 16 (over z, core).
Axes of the slice: x: 4, y: 8, z: 8, core: 2. Of those that a mesh axis runs over, the one named last changes fastest.
Arguments:
- queries: bfloat16 [2048, 8192], P('seq', 'head'), may hold values from -6 to 6
- keys: bfloat16 [2048, 1024], P('seq'), may hold values from -6 to 6
- values: bfloat16 [2048, 1024], P('seq'), may hold values from -6 to 6
- vertical: int32 [64, 8], replicated, may hold values from -1 to 31, as said below
- slash: int32 [64, 8], replicated, may hold values from -1 to 31, as said below
- plan: int32 [64], replicated, may hold values from 0 to 63, each once
Outputs:
- attended: bfloat16 [2048, 8192], P('seq', 'head')
Inputs may be any that keep to these rules, and one draw needn't show every extreme that they name: `vertical`: entries of 0 or more name key blocks of 64 positions; -1 marks an unused entry, and every row has at least one used entry. `slash`: entries of 0 or more are offsets back from a query's own block; -1 marks an unused entry; the first entry of every row is 0. `plan`: A permutation of the query heads.
All inputs are finite; a program needn't handle non-finite values.
Results may differ from a plain program's by a relative error of at most 0.0044.
Values may be sent and summed in bfloat16 or wider, within the bound.
A program may use at most 64 MiB of HBM per device.

v0:
```python
import jax
import jax.numpy as jnp
from jax import lax
from jax.sharding import PartitionSpec as P

HD = 128
QH = 64
KVH = 8
BLK = 64
floor_value = -1e30


def block_mask(query_blocks, key_blocks, vertical_rows, slash_rows, query_pos, key_pos):
    vertical_hit = jnp.any(vertical_rows[:, :, None] == key_blocks[None, None, :], axis=1)
    distance = query_blocks[:, None] - key_blocks[None, :]
    slash_hit = jnp.zeros((slash_rows.shape[0],) + distance.shape, jnp.bool_)
    for column in range(slash_rows.shape[1]):
        slash_hit = slash_hit | (slash_rows[:, column][:, None, None] == distance[None])
    causal = key_pos[None, :] <= query_pos[:, None]
    return causal[None] & (vertical_hit[:, None, :] | slash_hit)


def attend(carried, query_group, key_group, value_group, allowed, score_scale):
    max_old, totals_old, sums_old = carried
    scores = (
        jnp.einsum("qgh,kgh->gqk", query_group, key_group, preferred_element_type=jnp.float32)
        * score_scale
    )
    masked = jnp.where(allowed, scores, floor_value)
    max_new = jnp.maximum(max_old, jnp.max(masked, axis=2))
    weights = jnp.exp(masked - max_new[:, :, None])
    totals_new = jnp.sum(weights, axis=2)
    mixture = jnp.einsum(
        "gqk,kgh->qgh",
        weights.astype(jnp.bfloat16),
        value_group,
        preferred_element_type=jnp.float32,
    )
    return (max_new, totals_new, mixture)


def per_device(queries, keys, values, vertical, slash, plan):
    slot_count = plan.shape[0] // lax.axis_size("head")
    query_len = queries.shape[0]
    key_len = keys.shape[0]
    group_size = QH // KVH
    my_heads = lax.dynamic_slice_in_dim(plan, lax.axis_index("head") * slot_count, slot_count)
    kv_index = my_heads // group_size
    slot_column = jnp.arange(slot_count, dtype=jnp.int32)
    key_pick = jnp.take(keys.reshape(key_len, KVH, HD), kv_index, axis=1).reshape(
        key_len, slot_count * HD
    )
    value_pick = jnp.take(values.reshape(key_len, KVH, HD), kv_index, axis=1).reshape(
        key_len, slot_count * HD
    )
    gathered = lax.all_gather(queries, "head", axis=1, tiled=True)
    query_sel = jnp.take(gathered.reshape(query_len, QH, HD), my_heads, axis=1)
    vertical_sel = jnp.take(vertical, my_heads, axis=0)
    slash_sel = jnp.take(slash, my_heads, axis=0)
    query_pos = lax.axis_index("seq") * query_len + jnp.arange(query_len, dtype=jnp.int32)
    query_blocks = query_pos // BLK
    score_scale = HD ** (-0.5)

    def select_rows(rows):
        return jnp.take(rows.reshape(rows.shape[0], slot_count, HD), slot_column, axis=1)

    initial = (
        jnp.full((slot_count, query_len), floor_value, jnp.float32),
        jnp.zeros((slot_count, query_len), jnp.float32),
        jnp.zeros((query_len, slot_count, HD), jnp.float32),
    )
    key_piece = select_rows(lax.all_gather(key_pick, "seq", axis=0, tiled=True))
    value_piece = select_rows(lax.all_gather(value_pick, "seq", axis=0, tiled=True))
    piece_len = key_piece.shape[0]
    key_pos = jnp.arange(piece_len, dtype=jnp.int32)
    allowed = block_mask(query_blocks, key_pos // BLK, vertical_sel, slash_sel, query_pos, key_pos)
    max_parts = []
    total_parts = []
    sum_parts = []
    for lead in range(0, slot_count, 2):
        previous = (
            initial[0][lead : lead + 2],
            initial[1][lead : lead + 2],
            initial[2][:, lead : lead + 2],
        )
        updated = attend(
            previous,
            query_sel[:, lead : lead + 2],
            key_piece[:, lead : lead + 2],
            value_piece[:, lead : lead + 2],
            allowed[lead : lead + 2],
            score_scale,
        )
        max_parts.append(updated[0])
        total_parts.append(updated[1])
        sum_parts.append(updated[2])
    output = (
        jnp.concatenate(sum_parts, axis=1)
        / jnp.transpose(jnp.concatenate(total_parts, axis=0))[:, :, None]
    )
    return output.reshape(query_len, slot_count * HD).astype(jnp.bfloat16)


def solution(mesh):
    in_specs = (P("seq", "head"), P("seq", None), P("seq", None), P(), P(), P())
    out_specs = P("seq", "head")
    return jax.shard_map(
        per_device, mesh=mesh, in_specs=in_specs, out_specs=out_specs, check_vma=False
    )
```

profile of v0, /device:TPU:16, one launch (start us, length us, event | category | flops | bytes accessed | tf_op | source)
XLA Modules:
  0.0 250.0 jit_solution(17985091205724103392)
XLA Ops:
  6.5 0.0 copy-start
  6.5 0.0 all-gather.6.cloned.1.call-start
  6.5 0.7 all-gather.6.cloned.1.call-update
  7.3 0.0 all-gather.4.cloned.1.call-start
  7.3 0.7 compare_and_fusion
  8.1 0.0 copy-done
  8.1 0.6 gather_fusion.5
  8.7 0.9 copy_bitcast_fusion.1
  9.6 0.6 gather_fusion.1
  10.2 0.1 select_bitcast_fusion.3
  10.3 0.6 copy.48
  10.9 0.0 all-gather.4.cloned.1.call-update
  10.9 0.0 all-gather.8.cloned.1.call-start
  11.0 0.6 copy.49
  11.6 0.0 all-gather.8.cloned.1.call-update
  11.7 0.8 copy.28
  12.4 0.8 copy.29
  13.2 0.6 gather_fusion.3
  13.8 0.6 gather_fusion.4
  14.4 0.1 broadcast_select_fusion.4
  14.5 0.3 slice_reduce_fusion.7
  14.8 0.2 compare_reduce_fusion
  14.9 0.1 iota_compare_fusion
  15.1 0.1 broadcast_subtract_fusion
  15.2 2.2 or_and_fusion
  17.4 38.6 %all-gather.6.cloned.1.call-done = bf16[64,8192]{1,0:T(8,128)(2,1)} async-done(((bf16[64,512]{1,0:T(8,128)(2,1)}), bf16[64,8192]{1,0:T(8,128)(2,1)}) %all-gather.6.cloned.1.call-update) | async-done | bytes 1048592 | tf_op jit(solution)/shard_map/all_gather | solution.py:56
  56.0 1.5 copy_bitcast_fusion
  57.5 0.6 gather_fusion
  58.1 82.0 %all-gather.4.cloned.1.call-done = bf16[2048,512]{1,0:T(8,128)(2,1)} async-done(((bf16[64,512]{1,0:T(8,128)(2,1)}), bf16[2048,512]{1,0:T(8,128)(2,1)}) %all-gather.4.cloned.1.call-update) | async-done | bytes 2097168 | tf_op jit(solution)/shard_map/all_gather | solution.py:73
  140.1 3.9 %copy.26 = bf16[2048,512]{0,1:T(8,128)(2,1)} copy(bf16[2048,512]{1,0:T(8,128)(2,1)} %all-gather.4.cloned.1.call-done) | data formatting | bytes 4194304 | tf_op jit(solution)/shard_map/all_gather | solution.py:73
  144.1 3.0 %copy.27 = bf16[2048,4,128]{2,0,1:T(8,128)(2,1)S(1)} copy(bf16[2048,4,128]{0,2,1:T(8,128)(2,1)} %bitcast.53) | data formatting | bytes 4194304 | tf_op jit(solution)/shard_map/reshape | solution.py:65
  147.1 76.9 %all-gather.8.cloned.1.call-done = bf16[2048,512]{1,0:T(8,128)(2,1)} async-done(((bf16[64,512]{1,0:T(8,128)(2,1)}), bf16[2048,512]{1,0:T(8,128)(2,1)}) %all-gather.8.cloned.1.call-update) | async-done | bytes 2097168 | tf_op jit(solution)/shard_map/all_gather | solution.py:72
  224.1 4.0 %copy.33 = bf16[2048,512]{0,1:T(8,128)(2,1)} copy(bf16[2048,512]{1,0:T(8,128)(2,1)} %all-gather.8.cloned.1.call-done) | data formatting | bytes 4194304 | tf_op jit(solution)/shard_map/all_gather | solution.py:72
  228.0 4.0 %copy.34 = bf16[2048,4,128]{2,0,1:T(8,128)(2,1)} copy(bf16[2048,4,128]{0,2,1:T(8,128)(2,1)} %bitcast.54) | data formatting | bytes 4194304 | tf_op jit(solution)/shard_map/reshape | solution.py:65
  232.0 2.1 gather_fusion.2
  234.1 0.0 copy-start.1
  234.1 3.9 %gather_fusion.6 = bf16[4,2048,128]{2,1,0:T(8,128)(2,1)} fusion(bf16[2048,4,128]{2,0,1:T(8,128)(2,1)} %copy.34, s32[1024]{0:T(1024)S(1)} %pad_clamp_fusion), kind=kCustom, calls=%fused_computation.4.clone | custom fusion | bytes 4194320 | tf_op jit(solution)/shard_map/jit(_take)/gather | solution.py:65
  238.0 0.0 copy-done.1
  238.0 2.0 select_bitcast_fusion.1
  240.0 0.6 fusion.23
  240.7 0.7 fusion.24
  241.3 0.3 fusion.8
  241.6 0.4 convolution_bitcast_fusion
  242.0 0.4 convolution_bitcast_fusion.1
  242.4 0.3 fusion.6
  242.8 0.7 copy_bitcast_fusion.3
  (11 shorter events, 0.1 us)
Async XLA Ops:
  6.5 1.5 copy-start
  6.5 49.5 %all-gather.6.cloned.1.call-start = ((), (), s32[]{:S(2)}) async-start(), calls=%async_computation.1 | async-start | bytes 1114112 | tf_op jit(solution)/shard_map/all_gather | solution.py:56
  7.3 132.9 %all-gather.4.cloned.1.call-start = ((), (), s32[]{:S(2)}) async-start(), calls=%async_computation | async-start | bytes 2162688 | tf_op jit(solution)/shard_map/all_gather | solution.py:73
  10.9 213.1 %all-gather.8.cloned.1.call-start = ((), (), s32[]{:S(2)}) async-start(), calls=%async_computation.2 | async-start | bytes 2162688 | tf_op jit(solution)/shard_map/all_gather | solution.py:72
  234.1 3.9 %copy-start.1 = (bf16[4,2048,128]{2,1,0:T(8,128)(2,1)S(1)}, bf16[4,2048,128]{2,1,0:T(8,128)(2,1)}, u32[]{:S(2)}) copy-start(bf16[4,2048,128]{2,1,0:T(8,128)(2,1)} %gather_fusion.2) | copy-start | bytes 6291460
Sparse Core Ops, SparseCore 0:
  9.5 46.4 all-gather.5
  59.2 80.8 all-gather.3
  143.3 80.7 all-gather.7
where the time goes:
time: 251 us; the launch traced here: 250 us
  waiting for transfers between devices  198 us (79%)
  local copies, waits for them, and re-layouts  29.3 us (12%)
  between operations  13.3 us (5%)
  other arithmetic  6.95 us (3%)
    all_gather x1, waiting for transfers between devices, per_device(): lax.all_gather(value_pick, 'seq', axis=0, tiled=True)  82 us
    all_gather x1, waiting for transfers between devices, per_device(): key_piece = select_rows(lax.all_gather(key_pick, 'seq', axis=0, tiled=True))  76.9 us
    all_gather x1, waiting for transfers between devices, per_device(): gathered = lax.all_gather(queries, 'head', axis=1, tiled=True)  38.6 us
    reshape x2, local copies, waits for them, and re-layouts, select_rows(): rows.reshape(rows.shape[0], slot_count, HD)  6.99 us
    gather x2, local copies, waits for them, and re-layouts, select_rows(): jnp.take(rows.reshape(rows.shape[0], slot_count, HD), slot_column, axis=1)  5.99 us
  transfers between devices with their start and end apart: 3, of which 3 were waited for; matrix products, arithmetic and copies ran while one was open for 8% of the time, Pallas kernels for 0%

commit v1 on v0

--- a/solution.py
+++ b/solution.py
@@ -1,3 +1,4 @@
+import functools
 import jax
 import jax.numpy as jnp
 from jax import lax
@@ -8,6 +9,18 @@
 KVH = 8
 BLK = 64
 floor_value = -1e30
+
+
+def shapes_check(load, along_axis):
+    return jnp.concatenate(
+        jax.lax.all_to_all(
+            jnp.stack([load] * jax.lax.axis_size(along_axis), axis=0), along_axis, 0, 0
+        ),
+        axis=1,
+    )
+
+
+_note_values = functools.partial(shapes_check, along_axis="head")
 
 
 def block_mask(query_blocks, key_blocks, vertical_rows, slash_rows, query_pos, key_pos):
@@ -53,7 +66,7 @@
     value_pick = jnp.take(values.reshape(key_len, KVH, HD), kv_index, axis=1).reshape(
         key_len, slot_count * HD
     )
-    gathered = lax.all_gather(queries, "head", axis=1, tiled=True)
+    gathered = _note_values(queries)
     query_sel = jnp.take(gathered.reshape(query_len, QH, HD), my_heads, axis=1)
     vertical_sel = jnp.take(vertical, my_heads, axis=0)
     slash_sel = jnp.take(slash, my_heads, axis=0)

time: 251 us -> 209 us (0.83)
  waiting for transfers between devices: 198 us -> 144 us
  starting transfers between devices: 0.08 us -> 10.5 us
    all_gather x1 -> x0, waiting for transfers between devices: 38.6 us -> none  [per_device(): gathered = lax.all_gather(queries, 'head', axis=1, tiled=True)]
    all_gather x1, waiting for transfers between devices: 82 us -> 45.1 us  [per_device(): lax.all_gather(value_pick, 'seq', axis=0, tiled=True)]
    all_to_all x0 -> x1, waiting for transfers between devices: none -> 22.3 us  [shapes_check(): jax.lax.all_to_all(jnp.stack([load] * jax.lax.axis_size(along_axis), axis...]
    all_to_all x0 -> x1, starting transfers between devices: none -> 10.4 us  [shapes_check(): jax.lax.all_to_all(jnp.stack([load] * jax.lax.axis_size(along_axis), axis...]
    another operation x0 -> x3, local copies, waits for them, and re-layouts: none -> 3.27 us  [the longest x1 1.92 us: shapes_check(): jnp.stack([load] * jax.lax.axis_size(along_axis), axis=0)]
where the time goes in v1:
time: 209 us
  waiting for transfers between devices  144 us (69%)
  local copies, waits for them, and re-layouts  31.1 us (15%)
  between operations  13.6 us (7%)
  starting transfers between devices  10.5 us (5%)
  other arithmetic  6.95 us (3%)
    all_gather x1, waiting for transfers between devices, per_device(): key_piece = select_rows(lax.all_gather(key_pick, 'seq', axis=0, tiled=True))  76.9 us
    all_gather x1, waiting for transfers between devices, per_device(): lax.all_gather(value_pick, 'seq', axis=0, tiled=True)  45.1 us
    all_to_all x1, waiting for transfers between devices, shapes_check(): jax.lax.all_to_all(jnp.stack([load] * jax.lax.axis_size(along_axis), axis...  22.3 us
    all_to_all x1, starting transfers between devices, shapes_check(): jax.lax.all_to_all(jnp.stack([load] * jax.lax.axis_size(along_axis), axis...  10.4 us
    reshape x2, local copies, waits for them, and re-layouts, select_rows(): rows.reshape(rows.shape[0], slot_count, HD)  6.99 us
    gather x2, local copies, waits for them, and re-layouts, select_rows(): jnp.take(rows.reshape(rows.shape[0], slot_count, HD), slot_column, axis=1)  5.99 us
  transfers between devices with their start and end apart: 3, of which 3 were waited for; matrix products, arithmetic and copies ran while one was open for 8% of the time, Pallas kernels for 0%

profile of v1, /device:TPU:16, one launch (start us, length us, event | category | flops | bytes accessed | tf_op | source)
XLA Modules:
  0.0 208.7 jit_solution(12668821328732007236)
XLA Ops:
  6.5 0.0 copy-start
  6.5 0.0 all-gather.3.cloned.1.call-start
  6.5 0.9 copy-done
  7.5 0.9 copy_bitcast_fusion
  8.4 0.0 copy-start.2
  8.4 0.7 compare_and_fusion
  9.2 0.0 copy-start.3
  9.2 0.6 gather_fusion.5
  9.8 0.6 gather_fusion.1
  10.3 0.1 select_bitcast_fusion.3
  10.4 0.6 copy.61
  11.1 0.0 all-gather.3.cloned.1.call-update
  11.1 0.0 all-gather.5.cloned.1.call-start
  11.1 0.6 copy.62
  11.8 0.1 all-gather.5.cloned.1.call-update
  11.8 1.9 stack.2
  13.7 10.4 %all-to-all-start = ((bf16[16,64,512]{2,1,0:T(8,128)(2,1)}), bf16[16,64,512]{2,1,0:T(8,128)(2,1)S(1)}, u32[]{:S(2)}, u32[]{:S(2)}) async-start(bf16[16,64,512]{2,1,0:T(8,128)(2,1)} %stack.2), calls=%async_computation | async-start | bytes 2097152 | tf_op jit(solution)/shard_map/all_to_all | solution.py:16
  24.2 0.0 copy-done.2
  24.2 0.1 copy.42
  24.3 0.0 copy-done.3
  24.3 0.1 copy.43
  24.4 0.6 gather_fusion.3
  24.9 0.6 gather_fusion.4
  25.5 0.1 broadcast_select_fusion.4
  25.6 0.3 slice_reduce_fusion.7
  25.9 0.2 compare_reduce_fusion
  26.1 0.1 iota_compare_fusion
  26.2 0.1 broadcast_subtract_fusion
  26.3 2.2 %or_and_fusion = pred[4,64,2048]{2,1,0:T(32,128)(4,1)S(1)} fusion(s32[64,2048]{1,0:T(8,128)S(1)} %broadcast_subtract_fusion, s32[4]{0:T(128)S(1)} %get-tuple-element.8, s32[4]{0:T(128)S(1)} %get-tuple-element.10, s32[4]{0:T(128)S(1)} %get-tuple-element.11, s32[4]{0:T(128)S(1)} %get-tuple-element.12, s32[4]{0:T(128)S(1)} %get-tuple-element.13, ...), kind=kLoop, calls=%fused_computation.13 | loop fusion | flops 8912896 | bytes 1187968 | tf_op jit(solution)/shard_map/and | solution.py:33
  28.6 22.3 %all-to-all-done = bf16[16,64,512]{2,1,0:T(8,128)(2,1)S(1)} async-done(((bf16[16,64,512]{2,1,0:T(8,128)(2,1)}), bf16[16,64,512]{2,1,0:T(8,128)(2,1)S(1)}, u32[]{:S(2)}, u32[]{:S(2)}) %all-to-all-start) | async-done | bytes 1048608 | tf_op jit(solution)/shard_map/all_to_all | solution.py:16
  50.8 0.6 copy.44
  51.4 0.7 reshape_reshape.3
  52.1 0.7 copy.45
  52.8 0.6 gather_fusion
  53.3 45.1 %all-gather.3.cloned.1.call-done = bf16[2048,512]{1,0:T(8,128)(2,1)} async-done(((bf16[64,512]{1,0:T(8,128)(2,1)}), bf16[2048,512]{1,0:T(8,128)(2,1)}) %all-gather.3.cloned.1.call-update) | async-done | bytes 2097168 | tf_op jit(solution)/shard_map/all_gather | solution.py:86
  98.5 3.9 %copy.40 = bf16[2048,512]{0,1:T(8,128)(2,1)} copy(bf16[2048,512]{1,0:T(8,128)(2,1)} %all-gather.3.cloned.1.call-done) | data formatting | bytes 4194304 | tf_op jit(solution)/shard_map/all_gather | solution.py:86
  102.4 3.0 %copy.41 = bf16[2048,4,128]{2,0,1:T(8,128)(2,1)S(1)} copy(bf16[2048,4,128]{0,2,1:T(8,128)(2,1)} %bitcast.49) | data formatting | bytes 4194304 | tf_op jit(solution)/shard_map/reshape | solution.py:78
  105.5 76.9 %all-gather.5.cloned.1.call-done = bf16[2048,512]{1,0:T(8,128)(2,1)} async-done(((bf16[64,512]{1,0:T(8,128)(2,1)}), bf16[2048,512]{1,0:T(8,128)(2,1)}) %all-gather.5.cloned.1.call-update) | async-done | bytes 2097168 | tf_op jit(solution)/shard_map/all_gather | solution.py:85
  182.4 4.0 %copy.48 = bf16[2048,512]{0,1:T(8,128)(2,1)} copy(bf16[2048,512]{1,0:T(8,128)(2,1)} %all-gather.5.cloned.1.call-done) | data formatting | bytes 4194304 | tf_op jit(solution)/shard_map/all_gather | solution.py:85
  186.4 4.0 %copy.49 = bf16[2048,4,128]{2,0,1:T(8,128)(2,1)} copy(bf16[2048,4,128]{0,2,1:T(8,128)(2,1)} %bitcast.50) | data formatting | bytes 4194304 | tf_op jit(solution)/shard_map/reshape | solution.py:78
  190.3 2.1 %gather_fusion.2 = bf16[4,2048,128]{2,1,0:T(8,128)(2,1)} fusion(bf16[2048,4,128]{2,0,1:T(8,128)(2,1)S(1)} %copy.41, s32[1024]{0:T(1024)S(1)} %pad_clamp_fusion), kind=kCustom, calls=%fused_computation.1.clone | custom fusion | bytes 4194320 | tf_op jit(solution)/shard_map/jit(_take)/gather | solution.py:78
  192.4 0.0 copy-start.1
  192.4 3.9 %gather_fusion.6 = bf16[4,2048,128]{2,1,0:T(8,128)(2,1)} fusion(bf16[2048,4,128]{2,0,1:T(8,128)(2,1)} %copy.49, s32[1024]{0:T(1024)S(1)} %pad_clamp_fusion), kind=kCustom, calls=%fused_computation.4.clone | custom fusion | bytes 4194320 | tf_op jit(solution)/shard_map/jit(_take)/gather | solution.py:78
  196.3 0.0 copy-done.1
  196.3 2.0 select_bitcast_fusion.1
  198.4 0.6 fusion.23
  199.0 0.7 fusion.24
  199.7 0.3 fusion.8
  200.0 0.4 convolution_bitcast_fusion
  200.4 0.4 convolution_bitcast_fusion.1
  200.8 0.3 fusion.6
  201.1 0.7 copy_bitcast_fusion.2
  (10 shorter events, 0.1 us)
Async XLA Ops:
  6.5 0.9 copy-start
  6.5 92.0 %all-gather.3.cloned.1.call-start = ((), (), s32[]{:S(2)}) async-start(), calls=%async_computation.1 | async-start | bytes 2162688 | tf_op jit(solution)/shard_map/all_gather | solution.py:86
  8.4 15.8 %copy-start.2 = (s32[64,8]{0,1:T(8,128)S(1)}, s32[64,8]{0,1:T(8,128)}, u32[]{:S(2)}) copy-start(s32[64,8]{0,1:T(8,128)} %param.15) | copy-start | bytes 6148
  9.2 15.1 %copy-start.3 = (s32[64,8]{0,1:T(8,128)S(1)}, s32[64,8]{0,1:T(8,128)}, u32[]{:S(2)}) copy-start(s32[64,8]{0,1:T(8,128)} %param.16) | copy-start | bytes 6148
  11.1 171.3 %all-gather.5.cloned.1.call-start = ((), (), s32[]{:S(2)}) async-start(), calls=%async_computation.2 | async-start | bytes 2162688 | tf_op jit(solution)/shard_map/all_gather | solution.py:85
  13.7 37.1 %all-to-all-start = ((bf16[16,64,512]{2,1,0:T(8,128)(2,1)}), bf16[16,64,512]{2,1,0:T(8,128)(2,1)S(1)}, u32[]{:S(2)}, u32[]{:S(2)}) async-start(bf16[16,64,512]{2,1,0:T(8,128)(2,1)} %stack.2), calls=%async_computation | async-start | bytes 2097152 | tf_op jit(solution)/shard_map/all_to_all | solution.py:16
  192.4 3.9 %copy-start.1 = (bf16[4,2048,128]{2,1,0:T(8,128)(2,1)S(1)}, bf16[4,2048,128]{2,1,0:T(8,128)(2,1)}, u32[]{:S(2)}) copy-start(bf16[4,2048,128]{2,1,0:T(8,128)(2,1)} %gather_fusion.2) | copy-start | bytes 6291460
Sparse Core Ops, SparseCore 0:
  11.2 87.2 all-gather.2
  101.7 80.7 all-gather.4
